TPU v7x, 256 devices: a whole 4x4x8 slice. The times are simulated.
256 devices in a mesh: blk: 16 (over x_lo, z), rep: 16 (over y, x_hi, core).
Axes of the slice: x: 4 (x_hi: 2, x_lo: 2; x = x_hi * 2 + x_lo), y: 4, z: 8, core: 2. Of those that a mesh axis runs over, the one named last changes fastest.
Arguments:
- a_blocks: bfloat16 [48, 16, 6, 128, 128], P('blk', None, None, None, 'rep'), may hold values from -0.5 to 0.5
- a_cols: int32 [48, 16, 6], P('blk'), may hold values from 0 to 111, as said below
- b_blocks: bfloat16 [1792, 16, 3, 128, 128], P('blk', 'rep'), may hold values from -6 to 6
- b_cols: int32 [1792, 16, 3], P('blk', 'rep'), may hold values from 0 to 111, as said below
- c_cols: int32 [48, 16, 4], P(None, 'rep'), may hold values from 0 to 111, as said below
Outputs:
- c_blocks: float32 [48, 16, 4, 128, 128], P('blk', 'rep')
Inputs may be any that keep to these rules, and one draw needn't show every extreme that they name: `a_cols`: within each block row and panel the 6 entries are distinct. `b_cols`: within each block row and tile the 3 entries are distinct. `c_cols`: within each block row and tile the 4 entries are distinct.
All inputs are finite; a program needn't handle non-finite values.
Results may differ from a plain program's by a relative error of at most 0.0003.
Values may be sent and summed in bfloat16 or wider, within the bound.
A program may use at most 128 MiB of HBM per device.

v0:
```python
import math
import jax
import jax.numpy as jnp
from jax import lax
from jax.sharding import PartitionSpec as P


def select_blocks(chosen, chosen_cols, wanted):
    hits = chosen_cols[..., :, None] == wanted
    total = None
    for slot_t in range(chosen.shape[-3]):
        term = jnp.where(
            hits[..., slot_t, :, None, None],
            chosen[..., slot_t, None, :, :],
            jnp.zeros((), chosen.dtype),
        )
        total = term if total is None else total + term
    return total


def term_maker(slab, slab_cols, local_b, local_bcols, pattern):
    total_rows = slab.shape[0]
    slots = slab.shape[2]
    width = slab.shape[3]
    slab = slab.reshape(total_rows, slots, width, width)
    slab_cols = slab_cols.reshape(total_rows, slots)

    def partial_term(start, count):
        group = math.gcd(count, 2)

        def one_group(index):
            first = index * group
            left = lax.dynamic_slice_in_dim(slab, first, group, 0)
            where_k = lax.dynamic_slice_in_dim(slab_cols, first, group, 0)
            wanted = lax.dynamic_slice_in_dim(pattern, first, group, 0)
            chosen = jnp.take(local_b, where_k, axis=0)
            chosen_cols = jnp.take(local_bcols, where_k, axis=0)
            picked = select_blocks(chosen, chosen_cols, wanted[:, None, None, :])
            return jnp.einsum("isab,iscbd->icad", left, picked, preferred_element_type=jnp.float32)

        terms = lax.map(one_group, jnp.arange(count // group, dtype=jnp.int32))
        return terms.reshape(count, pattern.shape[1], width, width)

    return partial_term


def per_device(a_blocks, a_cols, b_blocks, b_cols, c_cols):
    own_rows = a_blocks.shape[0]
    local_b = b_blocks[:, 0]
    local_bcols = b_cols[:, 0]
    pattern = c_cols[:, 0]
    per_pattern = pattern.shape[1]
    whole = lax.all_gather(a_blocks, "rep", axis=4, tiled=True)
    slab, slab_cols = (
        lax.all_to_all(whole, "blk", split_axis=1, concat_axis=0, tiled=True),
        lax.all_to_all(a_cols, "blk", split_axis=1, concat_axis=0, tiled=True),
    )
    partial_term = term_maker(slab, slab_cols, local_b, local_bcols, pattern)
    mine = lax.psum_scatter(
        partial_term(jnp.int32(0), own_rows * lax.axis_size("blk")),
        "blk",
        scatter_dimension=0,
        tiled=True,
    )
    width = a_blocks.shape[3]
    return mine.reshape(own_rows, 1, per_pattern, width, width)


def solution(mesh):
    placed = (
        P("blk", None, None, None, "rep"),
        P("blk", None, None),
        P("blk", "rep", None, None, None),
        P("blk", "rep", None),
        P(None, "rep", None),
    )
    return jax.shard_map(
        per_device,
        mesh=mesh,
        in_specs=placed,
        out_specs=P("blk", "rep", None, None, None),
        check_vma=False,
    )
```

profile of v0, /device:TPU:1, one launch (start us, length us, event | category | flops | bytes accessed | tf_op | source)
XLA Modules:
  0.0 732.5 jit_solution(5404238477490479959)
XLA Ops:
  8.6 17.2 %all_to_all.30 = s32[3,16,6]{2,0,1:T(4,128)S(1)} all-to-all(s32[3,16,6]{2,0,1:T(4,128)S(1)} %copy.29), channel_id=1, replica_groups=mesh['blk'=16,'rep'=16] {'blk'}, dimensions={1} | all-to-all | bytes 2304 | tf_op jit(solution)/shard_map/all_to_all | solution.py:56
  25.8 75.8 %all-gather.2.cloned.1.call-done = bf16[3,16,6,128,128]{3,4,2,0,1:T(8,128)(2,1)} async-done(((bf16[3,16,6,128,8]{3,4,2,0,1:T(8,128)(2,1)}), bf16[3,16,6,128,128]{3,4,2,0,1:T(8,128)(2,1)}) %all-gather.2.cloned.1.call-update) | async-done | bytes 9437200 | tf_op jit(solution)/shard_map/all_gather | solution.py:53
  101.6 6.9 all-to-all-start.1
  108.8 210.0 %all-to-all-done.1 = bf16[3,16,6,128,128]{3,4,2,0,1:T(8,128)(2,1)} async-done(((bf16[3,16,6,128,128]{3,4,2,0,1:T(8,128)(2,1)}), bf16[3,16,6,128,128]{3,4,2,0,1:T(8,128)(2,1)}, u32[]{:S(2)}, u32[]{:S(2)}) %all-to-all-start.1) | async-done | bytes 9437216 | tf_op jit(solution)/shard_map/all_to_all | solution.py:55
  318.8 259.3 %while.10 = (s32[]{:T(128)}, f32[24,2,4,128,128]{4,3,2,1,0:T(8,128)}, s32[24]{0:T(128)S(1)}, s32[48,6]{1,0:T(8,128)S(1)}, s32[112,3]{1,0:T(8,128)S(1)}, /*index=...) while((s32[]{:T(128)}, ...), condition=%wide.region_1.2_spmd, body=%wide.region_0.1_spmd.sunk | while | flops 205849856 | bytes 13638623 | solution.py:41
  321.0 4.9 gather_fusion.1
  331.8 4.9 gather_fusion.1
  342.6 4.9 gather_fusion.1
  353.4 4.9 gather_fusion.1
  364.2 4.9 gather_fusion.1
  375.0 4.9 gather_fusion.1
  385.9 4.9 gather_fusion.1
  396.7 4.9 gather_fusion.1
  407.5 4.9 gather_fusion.1
  418.2 4.9 gather_fusion.1
  429.0 4.9 gather_fusion.1
  439.9 4.9 gather_fusion.1
  450.7 4.9 gather_fusion.1
  461.5 4.9 gather_fusion.1
  472.3 4.9 gather_fusion.1
  483.1 4.9 gather_fusion.1
  493.9 4.9 gather_fusion.1
  504.7 4.9 gather_fusion.1
  578.1 147.5 %reduce-scatter.2.cloned.1.call-done = f32[3,4,128,128]{3,2,1,0:T(8,128)} async-done(((f32[48,4,128,128]{3,2,1,0:T(8,128)}), f32[3,4,128,128]{3,2,1,0:T(8,128)}) %reduce-scatter.2.cloned.1.call-update) | async-done | bytes 786448 | tf_op jit(solution)/shard_map/reduce_scatter | solution.py:59
  (479 shorter events, 156.6 us)
Async XLA Ops:
  6.5 2.0 copy-start
  6.5 95.1 %all-gather.2.cloned.1.call-start = ((), (), s32[]{:S(2)}) async-start(), calls=%async_computation.3 | async-start | bytes 10027008 | tf_op jit(solution)/shard_map/all_gather | solution.py:53
  25.8 82.8 %copy-start.2 = (s32[112,1,3]{0,1,2:T(1,128)S(1)}, s32[112,1,3]{0,1,2:T(1,128)}, u32[]{:S(2)}) copy-start(s32[112,1,3]{0,1,2:T(1,128)} %param.10) | copy-start | bytes 4036
  25.8 82.9 %copy-start.1 = (s32[48,1,4]{0,2,1:T(4,128)S(1)}, s32[48,1,4]{0,2,1:T(4,128)}, u32[]{:S(2)}) copy-start(s32[48,1,4]{0,2,1:T(4,128)} %param.11) | copy-start | bytes 2308
  101.6 217.2 %all-to-all-start.1 = ((bf16[3,16,6,128,128]{3,4,2,0,1:T(8,128)(2,1)}), bf16[3,16,6,128,128]{3,4,2,0,1:T(8,128)(2,1)}, u32[]{:S(2)}, u32[]{:S(2)}) async-start(bf16[3,16,6,128,128]{3,4,2,0,1:T(8,128)(2,1)} %all-gather.2.cloned.1.call-done), calls=%async_computation.1 | async-start | bytes 18874368 | tf_op jit(solution)/shard_map/all_to_all | solution.py:55
  108.5 617.2 %reduce-scatter.2.cloned.1.call-start = ((), (), s32[]{:S(2)}) async-start(), calls=%async_computation.4 | async-start | bytes 13369344 | tf_op jit(solution)/shard_map/reduce_scatter | solution.py:59
Sparse Core Ops, SparseCore 0:
  10.0 91.5 all-gather.1
  578.3 147.3 reduce-scatter.1
where the time goes:
time: 735 us; the launch traced here: 733 us
  waiting for transfers between devices  433 us (59%)
  local copies, waits for them, and re-layouts  199 us (27%)
  matrix products  39 us (5%)
  blocking collectives  17.2 us (2%)
  loops' own time  16.8 us (2%)
  between operations  13.4 us (2%)
    all_to_all x1, waiting for transfers between devices, per_device(): lax.all_to_all(whole, 'blk', split_axis=1, concat_axis=0, tiled=True)  210 us
    reduce_scatter x1, waiting for transfers between devices, per_device(): lax.psum_scatter(partial_term(jnp.int32(0), own_rows * lax.axis_size('blk...  148 us
    gather x24, local copies, waits for them, and re-layouts, one_group(): chosen = jnp.take(local_b, where_k, axis=0)  118 us
    all_gather x1, waiting for transfers between devices, per_device(): whole = lax.all_gather(a_blocks, 'rep', axis=4, tiled=True)  75.8 us
    dot_general x24, matrix products, one_group(): jnp.einsum('isab,iscbd->icad', left, picked, preferred_element_type=jnp.f...  39 us
    dynamic_update_slice x48, local copies, waits for them, and re-layouts, partial_term(): terms = lax.map(one_group, jnp.arange(count // group, dtype=jnp.int32))  25.2 us
    broadcast_in_dim x120, local copies, waits for them, and re-layouts, select_blocks(): jnp.where(hits[..., slot_t, :, None, None], chosen[..., slot_t, None, :,...  18.6 us
    gather x72, local copies, waits for them, and re-layouts, one_group(): chosen_cols = jnp.take(local_bcols, where_k, axis=0)  17.6 us
  transfers between devices with their start and end apart: 3, of which 3 were waited for; matrix products, arithmetic and copies ran while one was open for 0% of the time, Pallas kernels for 0%

commit v1 on v0

--- a/solution.py
+++ b/solution.py
@@ -3,6 +3,13 @@
 import jax.numpy as jnp
 from jax import lax
 from jax.sharding import PartitionSpec as P
+
+
+def all_by_exchange(x, mesh_axis, dim):
+    devices = lax.axis_size(mesh_axis)
+    blocks = jnp.stack([x for _ in range(devices)])
+    blocks = lax.all_to_all(blocks, mesh_axis, split_axis=0, concat_axis=0)
+    return jnp.concatenate(blocks, axis=dim)
 
 
 def select_blocks(chosen, chosen_cols, wanted):
@@ -50,7 +57,7 @@
     local_bcols = b_cols[:, 0]
     pattern = c_cols[:, 0]
     per_pattern = pattern.shape[1]
-    whole = lax.all_gather(a_blocks, "rep", axis=4, tiled=True)
+    whole = all_by_exchange(a_blocks, "rep", 4)
     slab, slab_cols = (
         lax.all_to_all(whole, "blk", split_axis=1, concat_axis=0, tiled=True),
         lax.all_to_all(a_cols, "blk", split_axis=1, concat_axis=0, tiled=True),

time: 735 us -> 811 us (1.10)
  local copies, waits for them, and re-layouts: 199 us -> 238 us
  waiting for transfers between devices: 433 us -> 469 us
  starting transfers between devices: 6.93 us -> 24.7 us
  blocking collectives: 17.2 us -> 0 us
    all_to_all x0 -> x2, waiting for transfers between devices: none -> 107 us  [the longest x1 107 us: all_by_exchange(): blocks = lax.all_to_all(blocks, mesh_axis, split_axis=0, concat_axis=0)]
    all_gather x1 -> x0, waiting for transfers between devices: 75.8 us -> none  [per_device(): whole = lax.all_gather(a_blocks, 'rep', axis=4, tiled=True)]
    all_to_all x0 -> x2, local copies, waits for them, and re-layouts: none -> 22.6 us  [the longest x1 12.7 us: per_device(): lax.all_to_all(whole, 'blk', split_axis=1, concat_axis=0, tiled=True)]
    all_to_all x1 -> x0, blocking collectives: 17.2 us -> none  [per_device(): lax.all_to_all(a_cols, 'blk', split_axis=1, concat_axis=0, tiled=True)]
    all_to_all x0 -> x2, starting transfers between devices: none -> 16.9 us  [the longest x1 8.58 us: all_by_exchange(): blocks = lax.all_to_all(blocks, mesh_axis, split_axis=0, concat_axis=0)]
    reshape x0 -> x1, local copies, waits for them, and re-layouts: none -> 11.5 us  [all_by_exchange(): return jnp.concatenate(blocks, axis=dim)]
  transfers between devices with their start and end apart: 3 -> 4, of which waited for: 3 -> 3; matrix products, arithmetic and copies ran while one was open for 0% -> 3% of each run, Pallas kernels for 0% -> 0%
where the time goes in v1:
time: 811 us; the launch traced here: 808 us
  waiting for transfers between devices  469 us (58%)
  local copies, waits for them, and re-layouts  238 us (29%)
  matrix products  39 us (5%)
  starting transfers between devices  24.7 us (3%)
  loops' own time  17.3 us (2%)
  between operations  13.4 us (2%)
    all_to_all x1, waiting for transfers between devices, per_device(): lax.all_to_all(whole, 'blk', split_axis=1, concat_axis=0, tiled=True)  208 us
    reduce_scatter x1, waiting for transfers between devices, per_device(): lax.psum_scatter(partial_term(jnp.int32(0), own_rows * lax.axis_size('blk...  155 us
    gather x24, local copies, waits for them, and re-layouts, one_group(): chosen = jnp.take(local_b, where_k, axis=0)  118 us
    all_to_all x1, waiting for transfers between devices, all_by_exchange(): blocks = lax.all_to_all(blocks, mesh_axis, split_axis=0, concat_axis=0)  107 us
    dot_general x24, matrix products, one_group(): jnp.einsum('isab,iscbd->icad', left, picked, preferred_element_type=jnp.f...  39 us
    dynamic_update_slice x48, local copies, waits for them, and re-layouts, partial_term(): terms = lax.map(one_group, jnp.arange(count // group, dtype=jnp.int32))  25.2 us
    broadcast_in_dim x120, local copies, waits for them, and re-layouts, select_blocks(): jnp.where(hits[..., slot_t, :, None, None], chosen[..., slot_t, None, :,...  18.6 us
    gather x72, local copies, waits for them, and re-layouts, one_group(): chosen_cols = jnp.take(local_bcols, where_k, axis=0)  17.6 us
  transfers between devices with their start and end apart: 4, of which 3 were waited for; matrix products, arithmetic and copies ran while one was open for 3% of the time, Pallas kernels for 0%

profile of v1, /device:TPU:1, one launch (start us, length us, event | category | flops | bytes accessed | tf_op | source)
XLA Modules:
  0.0 808.1 jit_solution(17557104141131425933)
XLA Ops:
  6.5 7.0 stack.2
  13.5 8.6 %all-to-all-start.1 = ((bf16[16,3,16,6,128,8]{4,5,3,2,1,0:T(8,128)(2,1)}), bf16[16,3,16,6,128,8]{4,5,3,2,1,0:T(8,128)(2,1)}, u32[]{:S(2)}, u32[]{:S(2)}) async-start(bf16[16,3,16,6,128,8]{4,5,3,2,1,0:T(8,128)(2,1)} %stack.2), calls=%async_computation.1 | async-start | bytes 18874368 | tf_op jit(solution)/shard_map/all_to_all | solution.py:11
  22.8 106.6 %all-to-all-done.1 = bf16[16,3,16,6,128,8]{4,5,3,2,1,0:T(8,128)(2,1)} async-done(((bf16[16,3,16,6,128,8]{4,5,3,2,1,0:T(8,128)(2,1)}), bf16[16,3,16,6,128,8]{4,5,3,2,1,0:T(8,128)(2,1)}, u32[]{:S(2)}, u32[]{:S(2)}) %all-to-all-start.1) | async-done | bytes 9437216 | tf_op jit(solution)/shard_map/all_to_all | solution.py:11
  129.4 8.3 %all-to-all-start = ((s32[3,16,6]{2,0,1:T(4,128)}), s32[3,16,6]{2,0,1:T(4,128)S(1)}, u32[]{:S(2)}, u32[]{:S(2)}) async-start(s32[3,16,6]{2,0,1:T(4,128)} %copy.38), calls=%async_computation | async-start | bytes 65536 | tf_op jit(solution)/shard_map/all_to_all | solution.py:63
  137.7 10.0 %copy.53 = bf16[16,3,16,6,128,8]{4,5,0,3,2,1:T(8,128)(2,1)} copy(bf16[16,3,16,6,128,8]{4,5,3,2,1,0:T(8,128)(2,1)} %all-to-all-done.1) | data formatting | bytes 18874368 | tf_op jit(solution)/shard_map/all_to_all | solution.py:11
  147.7 11.5 %copy.43 = bf16[3,16,6,128,128]{3,4,2,0,1:T(8,128)(2,1)} copy(bf16[3,16,6,128,128]{3,4,2,1,0:T(8,128)(2,1)} %bitcast.61) | data formatting | bytes 18874368 | tf_op jit(solution)/shard_map/reshape | solution.py:12
  159.2 7.7 all-to-all-start.2
  167.2 207.7 %all-to-all-done.2 = bf16[3,16,6,128,128]{3,4,2,0,1:T(8,128)(2,1)} async-done(((bf16[3,16,6,128,128]{3,4,2,0,1:T(8,128)(2,1)}), bf16[3,16,6,128,128]{3,4,2,0,1:T(8,128)(2,1)}, u32[]{:S(2)}, u32[]{:S(2)}) %all-to-all-start.2) | async-done | bytes 9437216 | tf_op jit(solution)/shard_map/all_to_all | solution.py:62
  375.0 12.7 %copy.44 = bf16[3,16,6,128,128]{4,3,2,0,1:T(8,128)(2,1)} copy(bf16[3,16,6,128,128]{3,4,2,0,1:T(8,128)(2,1)} %all-to-all-done.2) | data formatting | bytes 18874368 | tf_op jit(solution)/shard_map/all_to_all | solution.py:62
  387.6 258.9 %while.10 = (s32[]{:T(128)}, f32[24,2,4,128,128]{4,3,2,1,0:T(8,128)}, s32[24]{0:T(128)S(1)}, s32[48,6]{1,0:T(8,128)S(1)}, s32[112,3]{1,0:T(8,128)S(1)}, /*index=...) while((s32[]{:T(128)}, ...), condition=%wide.region_1.2_spmd, body=%wide.region_0.1_spmd.sunk | while | flops 205849856 | bytes 13638623 | solution.py:48
  400.6 4.9 gather_fusion.1
  411.4 4.9 gather_fusion.1
  422.2 4.9 gather_fusion.1
  433.0 4.9 gather_fusion.1
  443.8 4.9 gather_fusion.1
  454.6 4.9 gather_fusion.1
  465.4 4.9 gather_fusion.1
  476.1 4.9 gather_fusion.1
  486.9 4.9 gather_fusion.1
  497.7 4.9 gather_fusion.1
  508.5 4.9 gather_fusion.1
  519.3 4.9 gather_fusion.1
  530.1 4.9 gather_fusion.1
  646.5 154.7 %reduce-scatter.2.cloned.1.call-done = f32[3,4,128,128]{3,2,1,0:T(8,128)} async-done(((f32[48,4,128,128]{3,2,1,0:T(8,128)}), f32[3,4,128,128]{3,2,1,0:T(8,128)}) %reduce-scatter.2.cloned.1.call-update) | async-done | bytes 786448 | tf_op jit(solution)/shard_map/reduce_scatter | solution.py:66
  (482 shorter events, 178.8 us)
Async XLA Ops:
  13.5 8.6 %copy-start = (s32[3,16,6]{1,2,0:T(8,128)S(1)}, s32[3,16,6]{1,2,0:T(8,128)}, u32[]{:S(2)}) copy-start(s32[3,16,6]{1,2,0:T(8,128)} %param.8) | copy-start | bytes 3460
  13.5 115.9 %all-to-all-start.1 = ((bf16[16,3,16,6,128,8]{4,5,3,2,1,0:T(8,128)(2,1)}), bf16[16,3,16,6,128,8]{4,5,3,2,1,0:T(8,128)(2,1)}, u32[]{:S(2)}, u32[]{:S(2)}) async-start(bf16[16,3,16,6,128,8]{4,5,3,2,1,0:T(8,128)(2,1)} %stack.2), calls=%async_computation.1 | async-start | bytes 18874368 | tf_op jit(solution)/shard_map/all_to_all | solution.py:11
  129.4 29.8 %all-to-all-start = ((s32[3,16,6]{2,0,1:T(4,128)}), s32[3,16,6]{2,0,1:T(4,128)S(1)}, u32[]{:S(2)}, u32[]{:S(2)}) async-start(s32[3,16,6]{2,0,1:T(4,128)} %copy.38), calls=%async_computation | async-start | bytes 65536 | tf_op jit(solution)/shard_map/all_to_all | solution.py:63
  159.2 7.8 copy-start.2
  159.2 7.9 copy-start.1
  159.2 215.8 %all-to-all-start.2 = ((bf16[3,16,6,128,128]{3,4,2,0,1:T(8,128)(2,1)}), bf16[3,16,6,128,128]{3,4,2,0,1:T(8,128)(2,1)}, u32[]{:S(2)}, u32[]{:S(2)}) async-start(bf16[3,16,6,128,128]{3,4,2,0,1:T(8,128)(2,1)} %copy.43), calls=%async_computation.2 | async-start | bytes 18874368 | tf_op jit(solution)/shard_map/all_to_all | solution.py:62
  166.9 634.3 %reduce-scatter.2.cloned.1.call-start = ((), (), s32[]{:S(2)}) async-start(), calls=%async_computation.4 | async-start | bytes 13369344 | tf_op jit(solution)/shard_map/reduce_scatter | solution.py:66
Sparse Core Ops, SparseCore 0:
  646.7 154.5 reduce-scatter.1
